TPU v7x, 32 devices: a whole 2x2x4 slice. The times are simulated.
32 devices in a mesh: group: 2 (over x), atom: 4 (over y, core), layer: 4 (over z).
Axes of the slice: x: 2, y: 2, z: 4, core: 2. Of those that a mesh axis runs over, the one named last changes fastest.
Arguments:
- activations: bfloat16 [256, 4, 2304], P('group', 'layer'), parts along dimension 0, may hold values from -6 to 6
- encoder: bfloat16 [8, 2304, 16384], P(('group', 'layer'), None, 'atom'), parts along dimension 0, may hold values from -0.0625 to 0.0625
- decoder: bfloat16 [32768, 4, 2304], P(('group', 'atom'), 'layer'), parts along dimension 0, may hold values from -1 to 1
- thresholds: float32 [32768], P(('group', 'atom')), parts along dimension 0, may hold values from 0.05 to 0.8
Outputs:
- codes: bfloat16 [256, 16384], P('group', 'atom'), parts along dimension 0
- reconstruction: bfloat16 [256, 4, 2304], P(('group', 'atom'), 'layer'), parts along dimension 0
There are 2 independent parts, one for each index of `group`. A program takes and returns all parts, laid end to end along the dimension named above; each array names one. Nothing has to cross between parts.
All inputs are finite; a program needn't handle non-finite values.
Results may differ from a plain program's by a relative error of at most 0.02.
The roundings to bfloat16 on the way count: a program that leaves them out, or rounds other values in their place, can miss the bound.
Values may be sent and summed in bfloat16 or wider, within the bound.
A program may use at most 128 MiB of HBM per device.

v0:
```python
import jax
import jax.numpy as jnp
from jax import lax
from jax.sharding import PartitionSpec as P

REFINES = 2


step_rate = 0.15
learn_rate = 0.001


def shards(activations, encoder, decoder, thresholds):
    rows_in = activations[:, 0, :]
    enc_local = encoder[0]
    dec_local = decoder[:, 0, :]
    tokens = rows_in.shape[0]
    atom_devices = lax.axis_size("atom")

    def spread(code_state):
        return code_state.astype(jnp.bfloat16)

    def residual_of(coded_now, weights):
        row_count = tokens // atom_devices
        partial_value = lax.psum_scatter(
            jnp.dot(coded_now, weights, preferred_element_type=jnp.float32).astype(jnp.bfloat16),
            "atom",
            scatter_dimension=0,
            tiled=True,
        ).astype(jnp.float32)
        own_rows = lax.dynamic_slice_in_dim(
            rows_in, lax.axis_index("atom") * row_count, row_count, 0
        ).astype(jnp.float32)
        residual = lax.all_gather(
            (own_rows - partial_value).astype(jnp.bfloat16), "atom", axis=0, tiled=True
        )
        return (residual, False)

    def refine(code_state, coded_now, weights):
        residual, transposed = residual_of(coded_now, weights)
        gradient = lax.psum(
            lax.dot_general(
                residual, weights, (((1,), (1,)), ((), ())), preferred_element_type=jnp.float32
            ).astype(jnp.bfloat16),
            "layer",
        ).astype(jnp.float32)
        code_state = jax.nn.relu(code_state + step_rate * gradient - step_rate * thresholds)
        return (code_state, spread(code_state))

    preact = lax.psum(
        jnp.dot(rows_in, enc_local, preferred_element_type=jnp.float32).astype(jnp.bfloat16),
        "layer",
    ).astype(jnp.float32)
    code_state = jax.nn.relu(preact - thresholds)
    coded_now = spread(code_state)
    for sweep in range(REFINES):
        code_state, coded_now = refine(code_state, coded_now, dec_local)
    residual, transposed = residual_of(coded_now, dec_local)
    update = lax.dot_general(
        coded_now, residual, (((0,), (0,)), ((), ())), preferred_element_type=jnp.float32
    )
    renewed = (dec_local.astype(jnp.float32) + learn_rate * (update / tokens)).astype(jnp.bfloat16)
    code_state, coded_now = refine(code_state, coded_now, renewed)
    rebuilt = lax.psum_scatter(
        jnp.dot(coded_now, renewed, preferred_element_type=jnp.float32).astype(jnp.bfloat16),
        "atom",
        scatter_dimension=0,
        tiled=True,
    )
    reconstruction = rebuilt[:, None, :]
    return (coded_now, reconstruction)


def solution(mesh):
    return jax.shard_map(
        shards,
        mesh=mesh,
        in_specs=(
            P("group", "layer", None),
            P(("group", "layer"), None, "atom"),
            P(("group", "atom"), "layer", None),
            P(("group", "atom")),
        ),
        out_specs=(P("group", "atom"), P(("group", "atom"), "layer", None)),
        check_vma=False,
    )
```

profile of v0, /device:TPU:0, one launch (start us, length us, event | category | flops | bytes accessed | tf_op | source)
XLA Modules:
  0.0 487.0 jit_solution(16662554394716441295)
XLA Ops:
  7.2 0.0 copy-start.4
  7.2 0.0 all-reduce.5.cloned.1.call-start
  7.2 10.2 %fusion.12 = bf16[128,4096]{1,0:T(8,128)(2,1)} fusion(bf16[1,2304,4096]{2,1,0:T(8,128)(2,1)} %param.5, bf16[128,1,2304]{2,0,1:T(8,128)(2,1)} %param.4), kind=kOutput, calls=%fused_computation.13 | convolution fusion | flops 2416443392 | bytes 20512768 | tf_op jit(solution)/shard_map/dot_general | solution.py:51
  17.4 0.0 all-reduce.5.cloned.1.call-update
  17.4 0.0 copy-start.3
  17.4 0.0 reduce-scatter.6.cloned.1.call-start
  17.5 54.6 %all-reduce.5.cloned.1.call-done = bf16[128,4096]{1,0:T(8,128)(2,1)} async-done(((bf16[128,4096]{1,0:T(8,128)(2,1)}), bf16[128,4096]{1,0:T(8,128)(2,1)}) %all-reduce.5.cloned.1.call-update) | async-done | bytes 1048592 | tf_op jit(solution)/shard_map/psum | solution.py:50
  72.1 0.0 copy-done.4
  72.1 10.1 %fusion.21 = bf16[128,2304]{1,0:T(8,128)(2,1)} fusion(bf16[4096,1,2304]{2,0,1:T(8,128)(2,1)} %param.6, bf16[128,4096]{1,0:T(8,128)(2,1)} %all-reduce.5.cloned.1.call-done, f32[4096]{0:T(1024)S(1)} %copy-done.4), kind=kOutput, calls=%fused_computation.17 | convolution fusion | flops 2418311168 | bytes 20529152 | tf_op jit(solution)/shard_map/dot_general | solution.py:26
  82.2 0.0 reduce-scatter.6.cloned.1.call-update
  82.3 0.0 all-reduce.7.cloned.1.call-start
  82.3 21.6 %reduce-scatter.6.cloned.1.call-done = bf16[32,2304]{1,0:T(8,128)(2,1)} async-done(((bf16[128,2304]{1,0:T(8,128)(2,1)}), bf16[32,2304]{1,0:T(8,128)(2,1)}) %reduce-scatter.6.cloned.1.call-update) | async-done | bytes 147472 | tf_op jit(solution)/shard_map/reduce_scatter | solution.py:25
  103.9 0.0 copy-done.3
  103.9 0.9 fusion.42
  104.8 7.1 %all_gather.12 = bf16[128,2304]{1,0:T(8,128)(2,1)S(1)} all-gather(bf16[32,2304]{1,0:T(8,128)(2,1)S(1)} %fusion.42), channel_id=1, replica_groups=mesh['group'=2,'atom'=4,'layer'=4] {'atom'}, dimensions={0}, use_global_device_ids=true | all-gather | bytes 737280 | tf_op jit(solution)/shard_map/all_gather | solution.py:34
  112.0 0.0 copy-start
  112.0 13.6 %fusion.15 = bf16[128,4096]{1,0:T(8,128)(2,1)} fusion(bf16[128,2304]{1,0:T(8,128)(2,1)S(1)} %all_gather.12, bf16[4096,1,2304]{2,0,1:T(8,128)(2,1)} %param.6), kind=kOutput, calls=%fused_computation.14 | convolution fusion | flops 2416443392 | bytes 20512768 | tf_op jit(solution)/shard_map/dot_general | solution.py:42
  125.5 0.0 all-reduce.7.cloned.1.call-update
  125.5 0.0 reduce-scatter.8.cloned.1.call-start
  125.6 52.3 %all-reduce.7.cloned.1.call-done = bf16[128,4096]{1,0:T(8,128)(2,1)} async-done(((bf16[128,4096]{1,0:T(8,128)(2,1)}), bf16[128,4096]{1,0:T(8,128)(2,1)}) %all-reduce.7.cloned.1.call-update) | async-done | bytes 1048592 | tf_op jit(solution)/shard_map/psum | solution.py:41
  177.9 0.0 copy-done
  177.9 10.4 %fusion.24 = bf16[128,2304]{1,0:T(8,128)(2,1)} fusion(bf16[4096,1,2304]{2,0,1:T(8,128)(2,1)} %param.6, bf16[128,4096]{1,0:T(8,128)(2,1)} %all-reduce.7.cloned.1.call-done, bf16[128,4096]{1,0:T(8,128)(2,1)S(1)} %copy-done, f32[4096]{0:T(1024)S(1)} %broadcast_multiply_fusion, f32[4096]{0:T(1024)S(1)} %copy-done.4), kind=kOutput, calls=%fused_computation.18 | convolution fusion | flops 2420932608 | bytes 21594112 | tf_op jit(solution)/shard_map/dot_general | solution.py:26
  188.3 0.0 reduce-scatter.8.cloned.1.call-update
  188.3 0.0 all-reduce.9.cloned.1.call-start
  188.4 21.5 %reduce-scatter.8.cloned.1.call-done = bf16[32,2304]{1,0:T(8,128)(2,1)} async-done(((bf16[128,2304]{1,0:T(8,128)(2,1)}), bf16[32,2304]{1,0:T(8,128)(2,1)}) %reduce-scatter.8.cloned.1.call-update) | async-done | bytes 147472 | tf_op jit(solution)/shard_map/reduce_scatter | solution.py:25
  209.9 0.9 fusion.43
  210.9 7.3 %all_gather.13 = bf16[128,2304]{1,0:T(8,128)(2,1)S(1)} all-gather(bf16[32,2304]{1,0:T(8,128)(2,1)S(1)} %fusion.43), channel_id=1, replica_groups=mesh['group'=2,'atom'=4,'layer'=4] {'atom'}, dimensions={0}, use_global_device_ids=true | all-gather | bytes 737280 | tf_op jit(solution)/shard_map/all_gather | solution.py:34
  218.2 0.0 copy-start.2
  218.2 13.6 %fusion.18 = bf16[128,4096]{1,0:T(8,128)(2,1)} fusion(bf16[128,2304]{1,0:T(8,128)(2,1)S(1)} %all_gather.13, bf16[4096,1,2304]{2,0,1:T(8,128)(2,1)} %param.6), kind=kOutput, calls=%fused_computation.15 | convolution fusion | flops 2416443392 | bytes 20512768 | tf_op jit(solution)/shard_map/dot_general | solution.py:42
  231.8 0.0 all-reduce.9.cloned.1.call-update
  231.8 0.0 reduce-scatter.10.cloned.1.call-start
  231.8 52.3 %all-reduce.9.cloned.1.call-done = bf16[128,4096]{1,0:T(8,128)(2,1)} async-done(((bf16[128,4096]{1,0:T(8,128)(2,1)}), bf16[128,4096]{1,0:T(8,128)(2,1)}) %all-reduce.9.cloned.1.call-update) | async-done | bytes 1048592 | tf_op jit(solution)/shard_map/psum | solution.py:41
  284.2 0.0 copy-done.2
  284.2 2.1 fusion.41
  286.3 9.8 %fusion.27 = bf16[128,2304]{1,0:T(8,128)(2,1)} fusion(bf16[128,4096]{1,0:T(8,128)(2,1)S(1)} %fusion.41, bf16[4096,1,2304]{2,0,1:T(8,128)(2,1)} %param.6), kind=kOutput, calls=%fused_computation.19 | convolution fusion | flops 2416214016 | bytes 20512768 | tf_op jit(solution)/shard_map/dot_general | solution.py:26
  296.1 0.0 reduce-scatter.10.cloned.1.call-update
  296.1 0.0 reduce-scatter.12.cloned.1.call-start
  296.2 21.6 %reduce-scatter.10.cloned.1.call-done = bf16[32,2304]{1,0:T(8,128)(2,1)} async-done(((bf16[128,2304]{1,0:T(8,128)(2,1)}), bf16[32,2304]{1,0:T(8,128)(2,1)}) %reduce-scatter.10.cloned.1.call-update) | async-done | bytes 147472 | tf_op jit(solution)/shard_map/reduce_scatter | solution.py:25
  317.8 1.0 fusion.44
  318.8 7.8 %all_gather.14 = bf16[128,2304]{1,0:T(8,128)(2,1)} all-gather(bf16[32,2304]{1,0:T(8,128)(2,1)S(1)} %fusion.44), channel_id=1, replica_groups=mesh['group'=2,'atom'=4,'layer'=4] {'atom'}, dimensions={0}, use_global_device_ids=true | all-gather | bytes 737280 | tf_op jit(solution)/shard_map/all_gather | solution.py:34
  326.6 12.9 %add_convert_fusion = bf16[4096,2304]{1,0:T(8,128)(2,1)} fusion(bf16[128,4096]{1,0:T(8,128)(2,1)S(1)} %fusion.41, bf16[128,2304]{1,0:T(8,128)(2,1)} %all_gather.14, bf16[4096,1,2304]{2,0,1:T(8,128)(2,1)} %param.6), kind=kOutput, calls=%fused_computation | convolution fusion | flops 2453667840 | bytes 39387136 | tf_op jit(solution)/shard_map/dot_general | solution.py:59
  339.4 9.8 %convolution_convert_fusion.2 = bf16[128,2304]{1,0:T(8,128)(2,1)} fusion(bf16[128,4096]{1,0:T(8,128)(2,1)S(1)} %fusion.41, bf16[4096,2304]{1,0:T(8,128)(2,1)} %add_convert_fusion), kind=kOutput, calls=%fused_computation.21 | convolution fusion | flops 2416214016 | bytes 20512768 | tf_op jit(solution)/shard_map/dot_general | solution.py:26
  349.2 0.0 reduce-scatter.12.cloned.1.call-update
  349.3 0.0 all-reduce.11.cloned.1.call-start
  349.3 22.6 %reduce-scatter.12.cloned.1.call-done = bf16[32,2304]{1,0:T(8,128)(2,1)} async-done(((bf16[128,2304]{1,0:T(8,128)(2,1)}), bf16[32,2304]{1,0:T(8,128)(2,1)}) %reduce-scatter.12.cloned.1.call-update) | async-done | bytes 147472 | tf_op jit(solution)/shard_map/reduce_scatter | solution.py:25
  371.9 1.0 fusion.45
  372.9 7.1 %all_gather.15 = bf16[128,2304]{1,0:T(8,128)(2,1)S(1)} all-gather(bf16[32,2304]{1,0:T(8,128)(2,1)S(1)} %fusion.45), channel_id=1, replica_groups=mesh['group'=2,'atom'=4,'layer'=4] {'atom'}, dimensions={0}, use_global_device_ids=true | all-gather | bytes 737280 | tf_op jit(solution)/shard_map/all_gather | solution.py:34
  380.0 13.5 %convolution_convert_fusion = bf16[128,4096]{1,0:T(8,128)(2,1)} fusion(bf16[128,2304]{1,0:T(8,128)(2,1)S(1)} %all_gather.15, bf16[4096,2304]{1,0:T(8,128)(2,1)} %add_convert_fusion), kind=kOutput, calls=%fused_computation.16 | convolution fusion | flops 2416443392 | bytes 20512768 | tf_op jit(solution)/shard_map/dot_general | solution.py:42
  393.5 0.0 all-reduce.11.cloned.1.call-update
  393.5 0.3 reduce-scatter.14.cloned.1.call-start
  393.8 52.0 %all-reduce.11.cloned.1.call-done = bf16[128,4096]{1,0:T(8,128)(2,1)} async-done(((bf16[128,4096]{1,0:T(8,128)(2,1)}), bf16[128,4096]{1,0:T(8,128)(2,1)}) %all-reduce.11.cloned.1.call-update) | async-done | bytes 1048592 | tf_op jit(solution)/shard_map/psum | solution.py:41
  445.9 2.8 maximum_convert_fusion
  448.7 0.0 copy-start.1
  448.7 10.2 %convolution_convert_fusion.1 = bf16[128,2304]{1,0:T(8,128)(2,1)} fusion(bf16[128,4096]{1,0:T(8,128)(2,1)S(1)} %maximum_convert_fusion, bf16[4096,2304]{1,0:T(8,128)(2,1)} %add_convert_fusion), kind=kOutput, calls=%fused_computation.20 | convolution fusion | flops 2416214016 | bytes 20512768 | tf_op jit(solution)/shard_map/dot_general | solution.py:65
  458.9 0.0 copy-done.1
  458.9 0.0 reduce-scatter.14.cloned.1.call-update
  458.9 21.6 %reduce-scatter.14.cloned.1.call-done = bf16[32,2304]{1,0:T(8,128)(2,1)} async-done(((bf16[128,2304]{1,0:T(8,128)(2,1)}), bf16[32,2304]{1,0:T(8,128)(2,1)}) %reduce-scatter.14.cloned.1.call-update) | async-done | bytes 147472 | tf_op jit(solution)/shard_map/reduce_scatter | solution.py:64
  (1 shorter events, 0.0 us)
Async XLA Ops:
  7.2 64.9 %copy-start.4 = (f32[4096]{0:T(1024)S(1)}, f32[4096]{0:T(1024)}, u32[]{:S(2)}) copy-start(f32[4096]{0:T(1024)} %param.7) | copy-start | bytes 49156
  7.2 64.9 %all-reduce.5.cloned.1.call-start = ((), (), s32[]{:S(2)}) async-start(), calls=%async_computation.5 | async-start | bytes 2097152 | tf_op jit(solution)/shard_map/psum | solution.py:50
  17.4 86.5 %copy-start.3 = (bf16[128,1,2304]{2,0,1:T(8,128)(2,1)S(1)}, bf16[128,1,2304]{2,0,1:T(8,128)(2,1)}, u32[]{:S(2)}) copy-start(bf16[128,1,2304]{2,0,1:T(8,128)(2,1)} %param.4) | copy-start | bytes 1769476
  17.4 86.5 %reduce-scatter.6.cloned.1.call-start = ((), (), s32[]{:S(2)}) async-start(), calls=%async_computation.6 | async-start | bytes 737280 | tf_op jit(solution)/shard_map/reduce_scatter | solution.py:25
  82.3 95.6 %all-reduce.7.cloned.1.call-start = ((), (), s32[]{:S(2)}) async-start(), calls=%async_computation.7 | async-start | bytes 2097152 | tf_op jit(solution)/shard_map/psum | solution.py:41
  112.0 65.9 %copy-start = (bf16[128,4096]{1,0:T(8,128)(2,1)S(1)}, bf16[128,4096]{1,0:T(8,128)(2,1)}, u32[]{:S(2)}) copy-start(bf16[128,4096]{1,0:T(8,128)(2,1)} %all-reduce.5.cloned.1.call-done) | copy-start | bytes 3145732
  125.5 84.4 %reduce-scatter.8.cloned.1.call-start = ((), (), s32[]{:S(2)}) async-start(), calls=%async_computation.8 | async-start | bytes 737280 | tf_op jit(solution)/shard_map/reduce_scatter | solution.py:25
  188.3 95.8 %all-reduce.9.cloned.1.call-start = ((), (), s32[]{:S(2)}) async-start(), calls=%async_computation.9 | async-start | bytes 2097152 | tf_op jit(solution)/shard_map/psum | solution.py:41
  218.2 65.9 %copy-start.2 = (bf16[128,4096]{1,0:T(8,128)(2,1)S(1)}, bf16[128,4096]{1,0:T(8,128)(2,1)}, u32[]{:S(2)}) copy-start(bf16[128,4096]{1,0:T(8,128)(2,1)} %all-reduce.7.cloned.1.call-done) | copy-start | bytes 3145732
  231.8 86.0 %reduce-scatter.10.cloned.1.call-start = ((), (), s32[]{:S(2)}) async-start(), calls=%async_computation.10 | async-start | bytes 737280 | tf_op jit(solution)/shard_map/reduce_scatter | solution.py:25
  296.1 75.8 %reduce-scatter.12.cloned.1.call-start = ((), (), s32[]{:S(2)}) async-start(), calls=%async_computation.11 | async-start | bytes 737280 | tf_op jit(solution)/shard_map/reduce_scatter | solution.py:25
  349.3 96.6 %all-reduce.11.cloned.1.call-start = ((), (), s32[]{:S(2)}) async-start(), calls=%async_computation.12 | async-start | bytes 2097152 | tf_op jit(solution)/shard_map/psum | solution.py:41
  393.5 87.0 %reduce-scatter.14.cloned.1.call-start = ((), (), s32[]{:S(2)}) async-start(), calls=%async_computation.13 | async-start | bytes 737280 | tf_op jit(solution)/shard_map/reduce_scatter | solution.py:64
  448.7 10.2 %copy-start.1 = (bf16[128,4096]{1,0:T(8,128)(2,1)}, bf16[128,4096]{1,0:T(8,128)(2,1)S(1)}, u32[]{:S(2)}) copy-start(bf16[128,4096]{1,0:T(8,128)(2,1)S(1)} %maximum_convert_fusion) | copy-start | bytes 3145732
Sparse Core Ops, SparseCore 0:
  17.5 54.5 all-reduce.4
  82.4 21.4 reduce-scatter.5
  125.7 52.1 all-reduce.6
  188.5 21.4 reduce-scatter.7
  231.9 52.1 all-reduce.8
  296.2 21.4 reduce-scatter.9
  349.4 22.4 reduce-scatter.11
  393.6 52.1 all-reduce.10
  459.0 21.4 reduce-scatter.13
where the time goes:
time: 488 us; the launch traced here: 487 us
  waiting for transfers between devices  320 us (66%)
  matrix products  114 us (23%)
  blocking collectives  29.4 us (6%)
  between operations  13.9 us (3%)
  other arithmetic  8.87 us (2%)
    psum x3, waiting for transfers between devices, refine(): lax.psum(lax.dot_general(residual, weights, (((1,), (1,)), ((), ())), pre...  157 us
    reduce_scatter x4, waiting for transfers between devices, residual_of(): lax.psum_scatter(jnp.dot(coded_now, weights, preferred_element_type=jnp.f...  87.3 us
    psum x1, waiting for transfers between devices, shards(): lax.psum(jnp.dot(rows_in, enc_local, preferred_element_type=jnp.float32)....  54.6 us
    dot_general x3, matrix products, refine(): lax.dot_general(residual, weights, (((1,), (1,)), ((), ())), preferred_el...  40.6 us
    dot_general x4, matrix products, residual_of(): jnp.dot(coded_now, weights, preferred_element_type=jnp.float32)  40.2 us
    all_gather x4, blocking collectives, residual_of(): lax.all_gather((own_rows - partial_value).astype(jnp.bfloat16), 'atom', a...  29.4 us
    reduce_scatter x1, waiting for transfers between devices, shards(): lax.psum_scatter(jnp.dot(coded_now, renewed, preferred_element_type=jnp.f...  21.6 us
    dot_general x1, matrix products, shards(): lax.dot_general(coded_now, residual, (((0,), (0,)), ((), ())), preferred_...  12.9 us
  transfers between devices with their start and end apart: 9, of which 9 were waited for; matrix products, arithmetic and copies ran while one was open for 0% of the time, Pallas kernels for 0%

commit v1 on v0

--- a/solution.py
+++ b/solution.py
@@ -1,6 +1,10 @@
+import functools
+
 import jax
 import jax.numpy as jnp
 from jax import lax
+from jax.experimental import pallas as pl
+from jax.experimental.pallas import tpu as pltpu
 from jax.sharding import PartitionSpec as P
 
 REFINES = 2
@@ -71,9 +75,280 @@
     return (coded_now, reconstruction)
 
 
+MESH = pl.DeviceIdType.MESH
+WIDE = 256
+LAG = (2, 4, 6, 8)
+
+
+def dot(a, b, dims):
+    return lax.dot_general(a, b, (dims, ((), ())), preferred_element_type=jnp.float32)
+
+
+def wide(x):
+    return x.astype(jnp.float32)
+
+
+def fused(chunks, tokens, acts, enc_hbm, dec_hbm, thr, codes_out, recon_out,
+          enc, dec, own, ends, parts, coded, state, acc, res, terms, core_in, y_out, y_in,
+          enc_sem, dec_sem, end_s, end_r, part_s, part_r, code_s, code_s2, code_r,
+          a_s, a_r):
+    z = lax.axis_index("layer")
+    a = lax.axis_index("atom")
+    rows = tokens // 4
+    core, y = lax.rem(a, 2), a // 2
+    mate = a + 1 - 2 * core
+    across = lax.rem(a + 2, 4)
+    diagonal = lax.rem(mate + 2, 4)
+    is_mid = z * (3 - z) != 0
+    is_end = z * (3 - z) == 0
+
+    def load_enc(c):
+        return pltpu.make_async_copy(
+            enc_hbm.at[:, pl.ds(pl.multiple_of(c * WIDE, WIDE), WIDE)], enc.at[c], enc_sem.at[c])
+
+    def load_dec(c):
+        return pltpu.make_async_copy(dec_hbm.at[c], dec.at[c], dec_sem.at[c])
+
+    @pl.loop(0, chunks)
+    def _(c):
+        load_enc(c).start()
+
+    @pl.loop(0, chunks)
+    def _(c):
+        load_dec(c).start()
+
+    barrier = pltpu.get_barrier_semaphore()
+    for step in (1, 2, 3):
+        pl.semaphore_signal(barrier, inc=1, device_id={"layer": lax.rem(z + step, 4)}, device_id_type=MESH)
+    for peer in (mate, across):
+        pl.semaphore_signal(barrier, inc=1, device_id={"atom": peer}, device_id_type=MESH)
+    pl.semaphore_wait(barrier, 5)
+
+    def to_layer(src, dst, send, recv, layer):
+        return pltpu.make_async_remote_copy(
+            src, dst, send, recv, device_id={"layer": layer}, device_id_type=MESH)
+
+    def to_atom(src, dst, k, atom):
+        return pltpu.make_async_remote_copy(
+            src, dst, a_s.at[k], a_r.at[k], device_id={"atom": atom}, device_id_type=MESH)
+
+    inner = 1 + z // 3
+    outer = 3 * (z - 1)
+    other = 3 - z
+
+    def end_copy(c):
+        return to_layer(own.at[c], ends.at[c], end_s.at[c], end_r.at[c], inner)
+
+    def part_copy(c):
+        return to_layer(own.at[c], parts.at[c], part_s.at[c], part_r.at[c], other)
+
+    def code_out(c):
+        return to_layer(coded.at[c], coded.at[c], code_s.at[c], code_r.at[c], outer)
+
+    def code_over(c):
+        return to_layer(coded.at[c], coded.at[c], code_s2.at[c], code_r.at[c], other)
+
+    def layer_phase(term, finish, first):
+        acc[...] = jnp.zeros_like(acc)
+
+        @pl.loop(0, chunks + LAG[3])
+        def _(s):
+            @pl.when(s < chunks)
+            def _():
+                own[s] = term(s).astype(jnp.bfloat16)
+
+                @pl.when(is_end)
+                def _():
+                    end_copy(s).start()
+
+            c1 = s - LAG[0]
+
+            @pl.when(is_mid & (c1 >= 0) & (c1 < chunks))
+            def _():
+                end_copy(c1).wait_recv()
+
+                @pl.when(z == 2 - lax.rem(c1, 2))
+                def _():
+                    own[c1] = (wide(own[c1]) + wide(ends[c1])).astype(jnp.bfloat16)
+                    part_copy(c1).start()
+
+            c2 = s - LAG[1]
+
+            @pl.when((c2 >= 0) & (c2 < chunks))
+            def _():
+                @pl.when(z == 1 + lax.rem(c2, 2))
+                def _():
+                    part_copy(c2).wait_recv()
+                    now = finish(c2, wide(own[c2]) + wide(ends[c2]) + wide(parts[c2]))
+                    state[c2] = now
+                    coded[c2] = now.astype(jnp.bfloat16)
+                    code_over(c2).start()
+                    code_out(c2).start()
+
+            c3 = s - LAG[2]
+
+            @pl.when((c3 >= 0) & (c3 < chunks))
+            def _():
+                @pl.when(z == 2 - lax.rem(c3, 2))
+                def _():
+                    code_over(c3).wait_recv()
+                    code_out(c3).start()
+
+            c4 = s - LAG[3]
+
+            @pl.when(c4 >= 0)
+            def _():
+                @pl.when(is_end)
+                def _():
+                    code_out(c4).wait_recv()
+
+                if first:
+                    load_dec(c4).wait()
+                acc[...] += dot(coded[c4], dec[c4], ((1,), (0,)))
+
+        @pl.loop(0, chunks)
+        def _(c):
+            @pl.when(is_end)
+            def _():
+                end_copy(c).wait_send()
+
+            @pl.when(is_mid)
+            def _():
+                code_out(c).wait_send()
+
+            @pl.when(z == 2 - lax.rem(c, 2))
+            def _():
+                part_copy(c).wait_send()
+
+            @pl.when(z == 1 + lax.rem(c, 2))
+            def _():
+                code_over(c).wait_send()
+
+    def block(r):
+        return pl.ds(pl.multiple_of(r * rows, rows), rows)
+
+    def atom_sum():
+        for r in range(4):
+            terms[r] = acc[r * rows:(r + 1) * rows].astype(jnp.bfloat16)
+        far = to_atom(terms.at[2 * (1 - y) + 1 - core], core_in.at[0], 0, mate)
+        near = to_atom(terms.at[2 * y + 1 - core], core_in.at[1], 1, mate)
+        far.start()
+        near.start()
+        far.wait_recv()
+        y_out[...] = (wide(terms[2 * (1 - y) + core]) + wide(core_in[0])).astype(jnp.bfloat16)
+        over = to_atom(y_out, y_in, 2, across)
+        over.start()
+        near.wait_recv()
+        over.wait_recv()
+        total = wide(terms[2 * y + core]) + wide(core_in[1]) + wide(y_in[...])
+        far.wait_send()
+        near.wait_send()
+        over.wait_send()
+        return total
+
+    def atom_stage():
+        total = atom_sum()
+        res[block(a)] = (wide(acts[block(a)]) - total).astype(jnp.bfloat16)
+        over = to_atom(res.at[block(a)], res.at[block(a)], 3, across)
+        near = to_atom(res.at[block(a)], res.at[block(a)], 4, mate)
+        far = to_atom(res.at[block(across)], res.at[block(across)], 5, mate)
+        over.start()
+        near.start()
+        over.wait_recv()
+        far.start()
+        near.wait_recv()
+        far.wait_recv()
+        over.wait_send()
+        near.wait_send()
+        far.wait_send()
+
+    def encode(c):
+        load_enc(c).wait()
+        return dot(acts[...], enc[c], ((1,), (0,)))
+
+    layer_phase(encode, lambda c, total: jnp.maximum(total - thr[c], 0.0), True)
+
+    def renew():
+        acc[...] = jnp.zeros_like(acc)
+
+        @pl.loop(0, chunks)
+        def _(c):
+            update = dot(coded[c], res[...], ((0,), (0,)))
+            dec[c] = (wide(dec[c]) + learn_rate * (update / tokens)).astype(jnp.bfloat16)
+            acc[...] += dot(coded[c], dec[c], ((1,), (0,)))
+
+    @pl.loop(0, REFINES + 2)
+    def _(p):
+        atom_stage()
+
+        @pl.when(p == REFINES)
+        def _():
+            renew()
+
+        @pl.when(p != REFINES)
+        def _():
+            layer_phase(
+                lambda c: dot(res[...], dec[c], ((1,), (1,))),
+                lambda c, total: jnp.maximum(
+                    state[c] + step_rate * total - step_rate * thr[c], 0.0),
+                False,
+            )
+
+    for c in range(chunks):
+        codes_out[:, c * WIDE:(c + 1) * WIDE] = coded[c]
+    recon_out[...] = atom_sum().astype(jnp.bfloat16)
+
+
+def fused_shards(activations, encoder, decoder, thresholds):
+    tokens, _, width = activations.shape
+    atoms = decoder.shape[0]
+    chunks = atoms // WIDE
+    rows = tokens // 4
+    bf16, f32 = jnp.bfloat16, jnp.float32
+    vmem = pl.BlockSpec(memory_space=pltpu.VMEM)
+    hbm = pl.BlockSpec(memory_space=pltpu.HBM)
+    dma = pltpu.SemaphoreType.DMA
+    codes, recon = pl.pallas_call(
+        functools.partial(fused, chunks, tokens),
+        out_shape=(
+            jax.ShapeDtypeStruct((tokens, atoms), bf16),
+            jax.ShapeDtypeStruct((rows, width), bf16),
+        ),
+        in_specs=[vmem, hbm, hbm, vmem],
+        out_specs=(vmem, vmem),
+        scratch_shapes=[
+            pltpu.VMEM((chunks, width, WIDE), bf16),
+            pltpu.VMEM((chunks, WIDE, width), bf16),
+            pltpu.VMEM((chunks, tokens, WIDE), bf16),
+            pltpu.VMEM((chunks, tokens, WIDE), bf16),
+            pltpu.VMEM((chunks, tokens, WIDE), bf16),
+            pltpu.VMEM((chunks, tokens, WIDE), bf16),
+            pltpu.VMEM((chunks, tokens, WIDE), f32),
+            pltpu.VMEM((tokens, width), f32),
+            pltpu.VMEM((tokens, width), bf16),
+            pltpu.VMEM((4, rows, width), bf16),
+            pltpu.VMEM((2, rows, width), bf16),
+            pltpu.VMEM((rows, width), bf16),
+            pltpu.VMEM((rows, width), bf16),
+        ] + [dma((chunks,))] * 9 + [dma((6,)), dma((6,))],
+        compiler_params=pltpu.CompilerParams(
+            collective_id=1, has_side_effects=True, vmem_limit_bytes=60 << 20),
+        cost_estimate=pl.CostEstimate(
+            flops=20 * tokens * atoms * width, bytes_accessed=4 * atoms * width, transcendentals=0),
+        name="crosscoder",
+    )(
+        activations[:, 0, :],
+        encoder[0],
+        decoder.reshape(chunks, WIDE, width),
+        thresholds.reshape(chunks, 1, WIDE),
+    )
+    return codes, recon[:, None, :]
+
+
 def solution(mesh):
+    fits = mesh.shape["atom"] == 4 and mesh.shape["layer"] == 4
     return jax.shard_map(
-        shards,
+        fused_shards if fits else shards,
         mesh=mesh,
         in_specs=(
             P("group", "layer", None),

time: 488 us -> 233 us (0.48)
  waiting for transfers between devices: 320 us -> 0 us
  Pallas kernels: 0 us -> 229 us
  matrix products: 114 us -> 0 us
  blocking collectives: 29.4 us -> 0 us
  between operations: 13.9 us -> 0.64 us
  other arithmetic: 8.87 us -> 0 us
    pallas_call x0 -> x1, Pallas kernels: none -> 229 us  [fused_shards(): pl.pallas_call(functools.partial(fused, chunks, tokens), out_shape=(jax.S...]
    psum x4 -> x0, waiting for transfers between devices: 211 us -> none  [the longest x3 157 us: refine(): lax.psum(lax.dot_general(residual, weights, (((1,), (1,)), ((), ())), pre...]
    dot_general x10 -> x0, matrix products: 114 us -> none  [the longest x3 40.6 us: refine(): lax.dot_general(residual, weights, (((1,), (1,)), ((), ())), preferred_el...]
    reduce_scatter x5 -> x0, waiting for transfers between devices: 109 us -> none  [the longest x4 87.3 us: residual_of(): lax.psum_scatter(jnp.dot(coded_now, weights, preferred_element_type=jnp.f...]
    all_gather x4 -> x0, blocking collectives: 29.4 us -> none  [residual_of(): lax.all_gather((own_rows - partial_value).astype(jnp.bfloat16), 'atom', a...]
    convert_element_type x6 -> x0, other arithmetic: 8.87 us -> none  [the longest x2 4.94 us: spread(): return code_state.astype(jnp.bfloat16)]
  transfers between devices with their start and end apart: 9 -> 0, of which waited for: 9 -> 0; matrix products, arithmetic and copies ran while one was open for 0% -> 0% of each run, Pallas kernels for 0% -> 0%
where the time goes in v1:
time: 233 us
  Pallas kernels  229 us (98%)
  local copies, waits for them, and re-layouts  3.87 us (2%)
    pallas_call x1, Pallas kernels, fused_shards(): pl.pallas_call(functools.partial(fused, chunks, tokens), out_shape=(jax.S...  229 us

profile of v1, /device:TPU:0, one launch (start us, length us, event | category | flops | bytes accessed | tf_op | source)
XLA Modules:
  0.0 233.1 jit_solution(9057212164879538844)
XLA Ops:
  0.6 228.6 %crosscoder.1 = (bf16[128,4096]{1,0:T(8,128)(2,1)}, bf16[32,2304]{1,0:T(8,128)(2,1)}) custom-call(bf16[128,2304]{1,0:T(8,128)(2,1)} %bitcast.8, bf16[2304,4096]{1,0:T(8,128)(2,1)} %bitcast.6, bf16[16,256,2304]{2,1,0:T(8,128)(2,1)} %bitcast.7, f32[16,1,256]{2,1,0:T(1,128)} %bitcast.9), custom_call_target="tpu_custom_call" | custom-call | flops 24159191040 | bytes 37748736 | tf_op jit(solution)/shard_map/crosscoder/pallas_call | solution.py:311
  229.2 2.3 copy.8
  231.5 1.6 copy.9

commit v2 on v1

--- a/solution.py
+++ b/solution.py
@@ -77,7 +77,8 @@
 
 MESH = pl.DeviceIdType.MESH
 WIDE = 256
-LAG = (2, 4, 6, 8)
+PIECES = 3
+LAG = (3, 6, 9, 13)
 
 
 def dot(a, b, dims):
@@ -98,7 +99,7 @@
     core, y = lax.rem(a, 2), a // 2
     mate = a + 1 - 2 * core
     across = lax.rem(a + 2, 4)
-    diagonal = lax.rem(mate + 2, 4)
+    span = acts.shape[1] // PIECES
     is_mid = z * (3 - z) != 0
     is_end = z * (3 - z) == 0
 
@@ -112,10 +113,6 @@
     @pl.loop(0, chunks)
     def _(c):
         load_enc(c).start()
-
-    @pl.loop(0, chunks)
-    def _(c):
-        load_dec(c).start()
 
     barrier = pltpu.get_barrier_semaphore()
     for step in (1, 2, 3):
@@ -155,6 +152,8 @@
         def _(s):
             @pl.when(s < chunks)
             def _():
+                if first:
+                    load_dec(s).start()
                 own[s] = term(s).astype(jnp.bfloat16)
 
                 @pl.when(is_end)
@@ -227,40 +226,62 @@
     def block(r):
         return pl.ds(pl.multiple_of(r * rows, rows), rows)
 
-    def atom_sum():
+    def cols(h):
+        return pl.ds(h * span, span)
+
+    def start_sum():
         for r in range(4):
             terms[r] = acc[r * rows:(r + 1) * rows].astype(jnp.bfloat16)
-        far = to_atom(terms.at[2 * (1 - y) + 1 - core], core_in.at[0], 0, mate)
-        near = to_atom(terms.at[2 * y + 1 - core], core_in.at[1], 1, mate)
-        far.start()
-        near.start()
-        far.wait_recv()
-        y_out[...] = (wide(terms[2 * (1 - y) + core]) + wide(core_in[0])).astype(jnp.bfloat16)
-        over = to_atom(y_out, y_in, 2, across)
-        over.start()
-        near.wait_recv()
-        over.wait_recv()
-        total = wide(terms[2 * y + core]) + wide(core_in[1]) + wide(y_in[...])
-        far.wait_send()
-        near.wait_send()
-        over.wait_send()
-        return total
+        sent = []
+        for h in range(PIECES):
+            far = to_atom(terms.at[2 * (1 - y) + 1 - core, :, cols(h)], core_in.at[0, :, cols(h)], 6 * h, mate)
+            far.start()
+            sent.append([far])
+        for h in range(PIECES):
+            near = to_atom(terms.at[2 * y + 1 - core, :, cols(h)], core_in.at[1, :, cols(h)], 6 * h + 1, mate)
+            near.start()
+            sent[h].append(near)
+        for h in range(PIECES):
+            sent[h][0].wait_recv()
+            y_out[:, cols(h)] = (
+                wide(terms[2 * (1 - y) + core, :, cols(h)]) + wide(core_in[0, :, cols(h)])
+            ).astype(jnp.bfloat16)
+            over = to_atom(y_out.at[:, cols(h)], y_in.at[:, cols(h)], 6 * h + 2, across)
+            over.start()
+            sent[h].append(over)
+        return sent
+
+    def piece_sum(sent, h):
+        sent[h][1].wait_recv()
+        sent[h][2].wait_recv()
+        return (wide(terms[2 * y + core, :, cols(h)]) + wide(core_in[1, :, cols(h)])
+                + wide(y_in[:, cols(h)]))
 
     def atom_stage():
-        total = atom_sum()
-        res[block(a)] = (wide(acts[block(a)]) - total).astype(jnp.bfloat16)
-        over = to_atom(res.at[block(a)], res.at[block(a)], 3, across)
-        near = to_atom(res.at[block(a)], res.at[block(a)], 4, mate)
-        far = to_atom(res.at[block(across)], res.at[block(across)], 5, mate)
-        over.start()
-        near.start()
-        over.wait_recv()
-        far.start()
-        near.wait_recv()
-        far.wait_recv()
-        over.wait_send()
-        near.wait_send()
-        far.wait_send()
+        sent = start_sum()
+        spread = []
+        for h in range(PIECES):
+            total = piece_sum(sent, h)
+            mine = res.at[block(a), cols(h)]
+            theirs = res.at[block(across), cols(h)]
+            res[block(a), cols(h)] = (wide(acts[block(a), cols(h)]) - total).astype(jnp.bfloat16)
+            over = to_atom(mine, mine, 6 * h + 3, across)
+            near = to_atom(mine, mine, 6 * h + 4, mate)
+            far = to_atom(theirs, theirs, 6 * h + 5, mate)
+            over.start()
+            near.start()
+            spread.append((over, near, far))
+        for over, near, far in spread:
+            over.wait_recv()
+            far.start()
+        for over, near, far in spread:
+            near.wait_recv()
+            far.wait_recv()
+        for h in range(PIECES):
+            for copy in sent[h]:
+                copy.wait_send()
+            for copy in spread[h]:
+                copy.wait_send()
 
     def encode(c):
         load_enc(c).wait()
@@ -294,9 +315,14 @@
                 False,
             )
 
+    sent = start_sum()
     for c in range(chunks):
         codes_out[:, c * WIDE:(c + 1) * WIDE] = coded[c]
-    recon_out[...] = atom_sum().astype(jnp.bfloat16)
+    for h in range(PIECES):
+        recon_out[:, cols(h)] = piece_sum(sent, h).astype(jnp.bfloat16)
+    for h in range(PIECES):
+        for copy in sent[h]:
+            copy.wait_send()
 
 
 def fused_shards(activations, encoder, decoder, thresholds):
@@ -330,7 +356,7 @@
             pltpu.VMEM((2, rows, width), bf16),
             pltpu.VMEM((rows, width), bf16),
             pltpu.VMEM((rows, width), bf16),
-        ] + [dma((chunks,))] * 9 + [dma((6,)), dma((6,))],
+        ] + [dma((chunks,))] * 9 + [dma((6 * PIECES,))] * 2,
         compiler_params=pltpu.CompilerParams(
             collective_id=1, has_side_effects=True, vmem_limit_bytes=60 << 20),
         cost_estimate=pl.CostEstimate(

time: 233 us -> 217 us (0.931)
  Pallas kernels: 229 us -> 212 us
    pallas_call x1, Pallas kernels: 229 us -> 212 us  [fused_shards(): pl.pallas_call(functools.partial(fused, chunks, tokens), out_shape=(jax.S...]
where the time goes in v2:
time: 217 us
  Pallas kernels  212 us (98%)
  local copies, waits for them, and re-layouts  3.87 us (2%)
    pallas_call x1, Pallas kernels, fused_shards(): pl.pallas_call(functools.partial(fused, chunks, tokens), out_shape=(jax.S...  212 us

profile of v2, /device:TPU:0, one launch (start us, length us, event | category | flops | bytes accessed | tf_op | source)
XLA Modules:
  0.0 216.7 jit_solution(14954876456067535123)
XLA Ops:
  0.6 212.2 %crosscoder.1 = (bf16[128,4096]{1,0:T(8,128)(2,1)}, bf16[32,2304]{1,0:T(8,128)(2,1)}) custom-call(bf16[128,2304]{1,0:T(8,128)(2,1)} %bitcast.8, bf16[2304,4096]{1,0:T(8,128)(2,1)} %bitcast.6, bf16[16,256,2304]{2,1,0:T(8,128)(2,1)} %bitcast.7, f32[16,1,256]{2,1,0:T(1,128)} %bitcast.9), custom_call_target="tpu_custom_call" | custom-call | flops 24159191040 | bytes 37748736 | tf_op jit(solution)/shard_map/crosscoder/pallas_call | solution.py:337
  212.8 2.3 %copy.8 = bf16[128,4096]{1,0:T(8,128)(2,1)} copy(bf16[128,4096]{1,0:T(8,128)(2,1)} %get-tuple-element.8) | data formatting | bytes 2097152
  215.1 1.6 copy.9

commit v3 on v2

--- a/solution.py
+++ b/solution.py
@@ -292,10 +292,10 @@
     def renew():
         acc[...] = jnp.zeros_like(acc)
 
-        @pl.loop(0, chunks)
+        @pl.loop(0, chunks, unroll=2)
         def _(c):
             update = dot(coded[c], res[...], ((0,), (0,)))
-            dec[c] = (wide(dec[c]) + learn_rate * (update / tokens)).astype(jnp.bfloat16)
+            dec[c] = (wide(dec[c]) + update * (learn_rate / tokens)).astype(jnp.bfloat16)
             acc[...] += dot(coded[c], dec[c], ((1,), (0,)))
 
     @pl.loop(0, REFINES + 2)

time: 217 us -> 214 us (0.986)
    pallas_call x1, Pallas kernels: 212 us -> 210 us  [fused_shards(): pl.pallas_call(functools.partial(fused, chunks, tokens), out_shape=(jax.S...]
where the time goes in v3:
time: 214 us
  Pallas kernels  210 us (98%)
  local copies, waits for them, and re-layouts  3.87 us (2%)
    pallas_call x1, Pallas kernels, fused_shards(): pl.pallas_call(functools.partial(fused, chunks, tokens), out_shape=(jax.S...  210 us

profile of v3, /device:TPU:0, one launch (start us, length us, event | category | flops | bytes accessed | tf_op | source)
XLA Modules:
  0.0 214.1 jit_solution(17337687046989146476)
XLA Ops:
  0.6 209.6 %crosscoder.1 = (bf16[128,4096]{1,0:T(8,128)(2,1)}, bf16[32,2304]{1,0:T(8,128)(2,1)}) custom-call(bf16[128,2304]{1,0:T(8,128)(2,1)} %bitcast.8, bf16[2304,4096]{1,0:T(8,128)(2,1)} %bitcast.6, bf16[16,256,2304]{2,1,0:T(8,128)(2,1)} %bitcast.7, f32[16,1,256]{2,1,0:T(1,128)} %bitcast.9), custom_call_target="tpu_custom_call" | custom-call | flops 24159191040 | bytes 37748736 | tf_op jit(solution)/shard_map/crosscoder/pallas_call | solution.py:337
  210.2 2.3 %copy.8 = bf16[128,4096]{1,0:T(8,128)(2,1)} copy(bf16[128,4096]{1,0:T(8,128)(2,1)} %get-tuple-element.8) | data formatting | bytes 2097152
  212.5 1.6 copy.9
